TPU v7x, 256 devices: a whole 4x4x8 slice. The times are simulated.
256 devices in a mesh: section: 2 (over y_lo), dp: 8 (over z), tensor: 16 (over x, y_hi, core).
Axes of the slice: x: 4, y: 4 (y_hi: 2, y_lo: 2; y = y_hi * 2 + y_lo), z: 8, core: 2. Of those that a mesh axis runs over, the one named last changes fastest.
Arguments:
- inputs: bfloat16 [2, 512, 6144], P(None, 'dp'), may hold values from -6 to 6
- cotangent: bfloat16 [2, 512, 6144], P(None, 'dp'), may hold values from -6 to 6
- gate_weight: bfloat16 [2, 6144, 6144], P('section', 'tensor', 'dp'), may hold values from -0.078125 to 0.078125
- up_weight: bfloat16 [2, 6144, 6144], P('section', 'tensor', 'dp'), may hold values from -0.078125 to 0.078125
- down_weight: bfloat16 [2, 6144, 6144], P('section', 'tensor', 'dp'), may hold values from -0.078125 to 0.078125
Outputs:
- section_out: bfloat16 [2, 2, 512, 6144], P('section', None, ('dp', 'tensor'))
- section_grad: bfloat16 [2, 2, 512, 6144], P('section', None, ('dp', 'tensor'))
- grad_gate: bfloat16 [2, 6144, 6144], P('section', 'tensor', 'dp')
- grad_up: bfloat16 [2, 6144, 6144], P('section', 'tensor', 'dp')
- grad_down: bfloat16 [2, 6144, 6144], P('section', 'tensor', 'dp')
All inputs are finite; a program needn't handle non-finite values.
Results may differ from a plain program's by a relative error of at most 0.03.
Values may be sent and summed in bfloat16 or wider, within the bound.
A program may use at most 128 MiB of HBM per device.

v0:
```python
import math

import jax
import jax.numpy as jnp
from jax import lax
from jax.sharding import PartitionSpec as P


def passed_along(block, axis, distance):
    devices = range(lax.axis_size(axis))
    route = [(i - distance, i) for i in devices if i - distance in devices]
    return lax.ppermute(block, axis, route)


def norm_parts(x):
    xf = x.astype(jnp.float32)
    r = lax.rsqrt(jnp.mean(xf * xf, axis=-1, keepdims=True) + 1e-05)
    return (xf, r, (xf * r).astype(jnp.bfloat16))


def hidden_parts(normed, w_gate, w_up):
    dims = (((1,), (1,)), ((), ()))
    a = lax.dot_general(normed, w_gate, dims, preferred_element_type=jnp.float32)
    b = lax.dot_general(normed, w_up, dims, preferred_element_type=jnp.float32)
    sig = jax.nn.sigmoid(a)
    return (a, b, (a * sig * b).astype(jnp.bfloat16))


def grad_parts(grad_full, a, b, w_gate, w_up, w_down):
    dims = (((1,), (1,)), ((), ()))
    dh = lax.dot_general(grad_full, w_down, dims, preferred_element_type=jnp.float32)
    sig = jax.nn.sigmoid(a)
    da = (dh * b * sig * (1.0 + a * (1.0 - sig))).astype(jnp.bfloat16)
    db = (dh * a * sig).astype(jnp.bfloat16)
    partial_value = jnp.dot(da, w_gate, preferred_element_type=jnp.float32)
    partial_value = partial_value + jnp.dot(db, w_up, preferred_element_type=jnp.float32)
    return (da, db, partial_value)


def input_grad(grad_rows, xf, r, dn):
    mixed = jnp.mean(dn * xf, axis=-1, keepdims=True)
    return (grad_rows.astype(jnp.float32) + r * (dn - xf * r * r * mixed)).astype(jnp.bfloat16)


def shards(inputs, cotangent, gate_weight, up_weight, down_weight):
    first = lax.axis_index("section") == 0
    micro, tok_dev, width = inputs.shape
    groups = lax.axis_size("tensor")
    share = tok_dev // groups
    start = lax.axis_index("tensor") * share
    w_gate, w_up, w_down = (
        lax.all_gather(gate_weight[0], "dp", axis=1, tiled=True),
        lax.all_gather(up_weight[0], "dp", axis=1, tiled=True),
        lax.all_gather(down_weight[0], "dp", axis=1, tiled=True),
    )
    saved = []
    outputs = []
    backs = []
    pieces = []
    received = jnp.zeros((tok_dev, width), jnp.bfloat16)
    for step in range(micro + 1):
        own = inputs[step] if step < micro else jnp.zeros((tok_dev, width), jnp.bfloat16)
        x_full = jnp.where(first, own, received)
        xf, r, normed = norm_parts(x_full)
        a, b, h = hidden_parts(normed, w_gate, w_up)
        total = lax.psum(
            jnp.dot(h, w_down, preferred_element_type=jnp.float32).astype(jnp.bfloat16), "tensor"
        ).astype(jnp.float32)
        y_full = (xf + total).astype(jnp.bfloat16)
        received = passed_along(y_full, "section", 1)
        saved.append((xf, r, normed, a, b, h))
        outputs.append(lax.dynamic_slice_in_dim(y_full, start, share, 0))
    returned = jnp.zeros((tok_dev, width), jnp.bfloat16)
    for turn in range(micro + 1):
        index = micro - turn
        own = (
            cotangent[micro - 1 - turn]
            if turn < micro
            else jnp.zeros((tok_dev, width), jnp.bfloat16)
        )
        grad_full = jnp.where(first, returned, own)
        xf, r, normed, a, b, h = saved[index]
        da, db, partial_value = grad_parts(grad_full, a, b, w_gate, w_up, w_down)
        dn = lax.psum(partial_value.astype(jnp.bfloat16), "tensor").astype(jnp.float32)
        dx_full = input_grad(grad_full, xf, r, dn)
        returned = passed_along(dx_full, "section", -1)
        backs.append(lax.dynamic_slice_in_dim(dx_full, start, share, 0))
        pieces.append((h, grad_full, da, db, normed))
    section_out = jnp.stack([jnp.where(first, outputs[m], outputs[m + 1]) for m in range(micro)])
    section_grad = jnp.stack(
        [jnp.where(first, backs[micro - m], backs[micro - 1 - m]) for m in range(micro)]
    )
    hidden_all = jnp.concatenate([item[0] for item in pieces], axis=0)
    grad_all = jnp.concatenate([item[1] for item in pieces], axis=0)
    pair_all = jnp.concatenate(
        [jnp.concatenate([item[2], item[3]], axis=1) for item in pieces], axis=0
    )
    normed_all = jnp.concatenate([item[4] for item in pieces], axis=0)
    scale = 1.0 / math.sqrt(micro * tok_dev * lax.axis_size("dp"))
    dims = (((0,), (0,)), ((), ()))
    ff_dev = w_gate.shape[0]
    first_part = lax.dot_general(normed_all, pair_all, dims, preferred_element_type=jnp.float32)
    second_part = lax.dot_general(grad_all, hidden_all, dims, preferred_element_type=jnp.float32)
    summed = lax.psum_scatter(
        (jnp.concatenate([first_part, second_part], axis=1) * scale).astype(jnp.bfloat16),
        "dp",
        scatter_dimension=0,
        tiled=True,
    ).astype(jnp.float32)
    sum_gate = summed[:, :ff_dev].T.astype(jnp.bfloat16)
    sum_up = summed[:, ff_dev : 2 * ff_dev].T.astype(jnp.bfloat16)
    sum_down = summed[:, 2 * ff_dev :].T.astype(jnp.bfloat16)
    return (section_out[None], section_grad[None], sum_gate[None], sum_up[None], sum_down[None])


def solution(mesh):
    in_specs = (
        P(None, "dp", None),
        P(None, "dp", None),
        P("section", "tensor", "dp"),
        P("section", "tensor", "dp"),
        P("section", "tensor", "dp"),
    )
    out_specs = (
        P("section", None, ("dp", "tensor"), None),
        P("section", None, ("dp", "tensor"), None),
        P("section", "tensor", "dp"),
        P("section", "tensor", "dp"),
        P("section", "tensor", "dp"),
    )
    return jax.shard_map(shards, mesh=mesh, in_specs=in_specs, out_specs=out_specs, check_vma=False)
```

profile of v0, /device:TPU:1, one launch (start us, length us, event | category | flops | bytes accessed | tf_op | source)
XLA Modules:
  0.0 1209.9 jit_solution(12036448908253176573)
XLA Ops:
  7.2 0.7 all-gather.7.cloned.1.call-update
  8.0 0.7 all-gather.9.cloned.1.call-update
  8.7 0.7 all-gather.11.cloned.1.call-update
  9.5 1.4 fusion.59
  10.9 1.4 convert_multiply_fusion.1
  12.3 61.0 %all-gather.7.cloned.1.call-done = bf16[1,384,6144]{2,1,0:T(8,128)(2,1)} async-done(((bf16[1,384,768]{2,1,0:T(8,128)(2,1)}), bf16[1,384,6144]{2,1,0:T(8,128)(2,1)}) %all-gather.7.cloned.1.call-update) | async-done | bytes 4718608 | tf_op jit(solution)/shard_map/all_gather | solution.py:52
  73.4 3.9 fusion.32
  77.3 56.3 %all-gather.9.cloned.1.call-done = bf16[1,384,6144]{2,1,0:T(8,128)(2,1)} async-done(((bf16[1,384,768]{2,1,0:T(8,128)(2,1)}), bf16[1,384,6144]{2,1,0:T(8,128)(2,1)}) %all-gather.9.cloned.1.call-update) | async-done | bytes 4718608 | tf_op jit(solution)/shard_map/all_gather | solution.py:53
  133.5 3.9 multiply_convert_fusion.9
  137.4 56.3 %all-gather.11.cloned.1.call-done = bf16[1,384,6144]{2,1,0:T(8,128)(2,1)} async-done(((bf16[1,384,768]{2,1,0:T(8,128)(2,1)}), bf16[1,384,6144]{2,1,0:T(8,128)(2,1)}) %all-gather.11.cloned.1.call-update) | async-done | bytes 4718608 | tf_op jit(solution)/shard_map/all_gather | solution.py:54
  193.7 4.3 convolution_convert_fusion.2
  198.1 143.1 %all-reduce.7.cloned.1.call-done = bf16[64,6144]{1,0:T(8,128)(2,1)} async-done(((bf16[64,6144]{1,0:T(8,128)(2,1)}), bf16[64,6144]{1,0:T(8,128)(2,1)}) %all-reduce.7.cloned.1.call-update) | async-done | bytes 786448 | tf_op jit(solution)/shard_map/psum | solution.py:66
  341.2 1.5 fusion.60
  342.7 2.5 collective-permute-start
  345.2 15.5 %collective-permute-done = bf16[64,6144]{1,0:T(8,128)(2,1)S(1)} collective-permute-done((bf16[64,6144]{1,0:T(8,128)(2,1)S(1)}, bf16[64,6144]{1,0:T(8,128)(2,1)S(1)}, u32[]{:S(2)}, u32[]{:S(2)}) %collective-permute-start) | collective-permute-done | bytes 786464 | tf_op jit(solution)/shard_map/ppermute | solution.py:12
  360.7 0.4 fusion.56
  361.1 0.2 fusion.47
  361.4 4.3 fusion.30
  365.7 1.6 multiply_convert_fusion.8
  367.3 1.9 convolution_convert_fusion.1
  369.3 145.2 %all-reduce.9.cloned.1.call-done = bf16[64,6144]{1,0:T(8,128)(2,1)} async-done(((bf16[64,6144]{1,0:T(8,128)(2,1)}), bf16[64,6144]{1,0:T(8,128)(2,1)}) %all-reduce.9.cloned.1.call-update) | async-done | bytes 786448 | tf_op jit(solution)/shard_map/psum | solution.py:66
  514.5 1.3 fusion.57
  515.8 2.7 collective-permute-start.1
  518.5 1.3 select_bitcast_fusion
  519.9 0.9 copy-done.10
  520.8 3.9 fusion.8
  524.7 9.2 collective-permute-done.1
  533.8 0.3 multiply_reduce_fusion
  534.2 0.2 multiply_convert_fusion
  534.4 1.6 fusion.16
  536.0 1.6 multiply_convert_fusion.5
  537.6 1.0 fusion.26
  538.6 1.9 fusion.1
  540.6 145.2 %all-reduce.11.cloned.1.call-done = bf16[64,6144]{1,0:T(8,128)(2,1)} async-done(((bf16[64,6144]{1,0:T(8,128)(2,1)}), bf16[64,6144]{1,0:T(8,128)(2,1)}) %all-reduce.11.cloned.1.call-update) | async-done | bytes 786448 | tf_op jit(solution)/shard_map/psum | solution.py:84
  685.8 1.6 fusion.49
  687.4 2.0 fusion.52
  689.4 1.4 collective-permute-start.2
  690.9 18.8 %collective-permute-done.2 = bf16[64,6144]{1,0:T(8,128)(2,1)S(1)} collective-permute-done((bf16[64,6144]{1,0:T(8,128)(2,1)S(1)}, bf16[64,6144]{1,0:T(8,128)(2,1)S(1)}, u32[]{:S(2)}, u32[]{:S(2)}) %collective-permute-start.2) | collective-permute-done | bytes 786464 | tf_op jit(solution)/shard_map/ppermute | solution.py:12
  709.7 1.4 bitcast_select_fusion
  711.1 4.0 multiply_convert_fusion.3
  715.2 1.0 fusion.24
  716.2 2.0 fusion.2
  718.2 142.3 %all-reduce.13.cloned.1.call-done = bf16[64,6144]{1,0:T(8,128)(2,1)} async-done(((bf16[64,6144]{1,0:T(8,128)(2,1)}), bf16[64,6144]{1,0:T(8,128)(2,1)}) %all-reduce.13.cloned.1.call-update) | async-done | bytes 786448 | tf_op jit(solution)/shard_map/psum | solution.py:84
  860.4 1.4 fusion.58
  861.9 1.7 fusion.55
  863.6 1.5 collective-permute-start.3
  865.1 4.3 convolution_convert_fusion
  869.4 14.3 %collective-permute-done.3 = bf16[64,6144]{1,0:T(8,128)(2,1)S(1)} collective-permute-done((bf16[64,6144]{1,0:T(8,128)(2,1)S(1)}, bf16[64,6144]{1,0:T(8,128)(2,1)S(1)}, u32[]{:S(2)}, u32[]{:S(2)}) %collective-permute-start.3) | collective-permute-done | bytes 786464 | tf_op jit(solution)/shard_map/ppermute | solution.py:12
  883.8 5.5 fusion.40
  889.4 1.6 multiply_convert_fusion.1
  891.0 7.9 fusion.34
  899.0 1.0 fusion.22
  900.0 1.9 fusion.3
  901.9 16.6 %fusion = bf16[6144,1152]{0,1:T(8,128)(2,1)} fusion(f32[6144,384]{0,1:T(8,128)} %fusion.40, f32[6144,768]{0,1:T(8,128)} %fusion.34), kind=kLoop, calls=%fused_computation.1 | loop fusion | flops 21233664 | bytes 42467328 | tf_op jit(solution)/shard_map/convert_element_type | solution.py:105
  918.6 1.3 fusion.62
  919.9 127.4 %all-reduce.15.cloned.1.call-done = (bf16[64,6144]{1,0:T(8,128)(2,1)}, bf16[64,6144]{1,0:T(8,128)(2,1)}) async-done(((bf16[64,6144]{1,0:T(8,128)(2,1)}, bf16[64,6144]{1,0:T(8,128)(2,1)}), (bf16[64,6144]{1,0:T(8,128)(2,1)}, bf16[64,6144]{1,0:T(8,128)(2,1)})) %all-reduce.15.cloned.1.call-update) | async-done | bytes 1572880 | tf_op jit(solution)/shard_map/psum | solution.py:66
  1047.3 1.3 convert_element_type.162
  1048.7 0.4 fusion.61
  1049.1 0.1 dynamic-slice.1
  1049.1 1.5 select_bitcast_fusion.2
  1050.7 0.7 maximum_bitcast_fusion.1
  1051.4 0.7 maximum_bitcast_fusion
  1052.1 148.6 %reduce-scatter.2.cloned.1.call-done = bf16[768,1152]{0,1:T(8,128)(2,1)} async-done(((bf16[6144,1152]{0,1:T(8,128)(2,1)}), bf16[768,1152]{0,1:T(8,128)(2,1)}) %reduce-scatter.2.cloned.1.call-update) | async-done | bytes 1769488 | tf_op jit(solution)/shard_map/reduce_scatter | solution.py:104
  1200.7 2.7 slice_bitcast_fusion
  (101 shorter events, 0.8 us)
Async XLA Ops:
  7.2 3.7 copy-start.6
  7.2 66.2 %all-gather.7.cloned.1.call-start = ((), (), s32[]{:S(2)}) async-start(), calls=%async_computation.6 | async-start | bytes 5308416 | tf_op jit(solution)/shard_map/all_gather | solution.py:52
  7.9 125.6 %all-gather.9.cloned.1.call-start = ((), (), s32[]{:S(2)}) async-start(), calls=%async_computation.7 | async-start | bytes 5308416 | tf_op jit(solution)/shard_map/all_gather | solution.py:53
  8.7 185.0 %all-gather.11.cloned.1.call-start = ((), (), s32[]{:S(2)}) async-start(), calls=%async_computation.8 | async-start | bytes 5308416 | tf_op jit(solution)/shard_map/all_gather | solution.py:54
  9.4 331.8 %all-reduce.7.cloned.1.call-start = ((), (), s32[]{:S(2)}) async-start(), calls=%async_computation.1 | async-start | bytes 1572864 | tf_op jit(solution)/shard_map/psum | solution.py:66
  12.3 121.2 %copy-start.2 = (bf16[64,6144]{1,0:T(8,128)(2,1)}, bf16[64,6144]{1,0:T(8,128)(2,1)S(1)}, u32[]{:S(2)}) copy-start(bf16[64,6144]{1,0:T(8,128)(2,1)S(1)} %get-tuple-element.13) | copy-start | bytes 2359300
  193.7 172.0 %slice-start.6 = ((s8[4718592]{0:T(1024)(128)(4,1)}), s8[524288]{0:T(1024)(128)(4,1)S(1)}, s32[]{:S(2)}) async-start(s8[4718592]{0:T(1024)(128)(4,1)} %bitcast.114), calls=%async_computation.16 | async-start | bytes 1048576
  198.0 316.4 %all-reduce.9.cloned.1.call-start = ((), (), s32[]{:S(2)}) async-start(), calls=%async_computation.2 | async-start | bytes 1572864 | tf_op jit(solution)/shard_map/psum | solution.py:66
  341.2 19.6 %copy-start.7 = (bf16[2,64,6144]{2,1,0:T(8,128)(2,1)S(1)}, bf16[2,64,6144]{2,1,0:T(8,128)(2,1)}, u32[]{:S(2)}) copy-start(bf16[2,64,6144]{2,1,0:T(8,128)(2,1)} %param.5) | copy-start | bytes 4718596
  342.7 2.6 copy-start.13
  342.7 23.0 %slice-start.7 = ((s8[4718592]{0:T(1024)(128)(4,1)}), s8[4194304]{0:T(1024)(128)(4,1)S(1)}, s32[]{:S(2)}) async-start(s8[4718592]{0:T(1024)(128)(4,1)} %bitcast.114), calls=%async_computation.17 | async-start | bytes 8388608
  342.7 18.0 %collective-permute-start = (bf16[64,6144]{1,0:T(8,128)(2,1)S(1)}, bf16[64,6144]{1,0:T(8,128)(2,1)S(1)}, u32[]{:S(2)}, u32[]{:S(2)}) collective-permute-start(bf16[64,6144]{1,0:T(8,128)(2,1)S(1)} %fusion.60), channel_id=1, source_target_pairs={{0,128},{1,129},{2,130},{3,131},{4,132},{5,133},{6,134},{7,135},{8... | collective-permute-start | bytes 2359304 | tf_op jit(solution)/shard_map/ppermute | solution.py:12
  361.1 6.1 slice-start.14
  361.3 4.3 copy-start
  361.4 5.9 slice-start.15
  367.3 167.1 %slice-start.8 = ((s8[4718592]{0:T(1024)(128)(4,1)}), s8[524288]{0:T(1024)(128)(4,1)S(1)}, s32[]{:S(2)}) async-start(s8[4718592]{0:T(1024)(128)(4,1)} %bitcast.116), calls=%async_computation.18 | async-start | bytes 1048576
  369.2 316.5 %all-reduce.11.cloned.1.call-start = ((), (), s32[]{:S(2)}) async-start(), calls=%async_computation.3 | async-start | bytes 1572864 | tf_op jit(solution)/shard_map/psum | solution.py:84
  515.8 8.9 copy-start.14
  515.8 18.6 %slice-start.9 = ((s8[4718592]{0:T(1024)(128)(4,1)}), s8[4194304]{0:T(1024)(128)(4,1)S(1)}, s32[]{:S(2)}) async-start(s8[4718592]{0:T(1024)(128)(4,1)} %bitcast.116), calls=%async_computation.19 | async-start | bytes 8388608
  515.8 18.0 %collective-permute-start.1 = (bf16[64,6144]{1,0:T(8,128)(2,1)S(1)}, bf16[64,6144]{1,0:T(8,128)(2,1)S(1)}, u32[]{:S(2)}, u32[]{:S(2)}) collective-permute-start(bf16[64,6144]{1,0:T(8,128)(2,1)S(1)} %fusion.57), channel_id=1, source_target_pairs={{0,128},{1,129},{2,130},{3,131},{4,132},{5,133},{6,134},{7,135},{8... | collective-permute-start | bytes 2359304 | tf_op jit(solution)/shard_map/ppermute | solution.py:12
  518.5 17.5 %slice-start = ((s8[4718592]{0:T(1024)(128)(4,1)}), s8[4194304]{0:T(1024)(128)(4,1)S(1)}, s32[]{:S(2)}) async-start(s8[4718592]{0:T(1024)(128)(4,1)} %bitcast.108), calls=%async_computation.10 | async-start | bytes 8388608
  519.9 0.9 copy-start.10
  524.7 11.3 slice-start.1
  534.4 1.6 copy-start.4
  540.5 319.9 %all-reduce.13.cloned.1.call-start = ((), (), s32[]{:S(2)}) async-start(), calls=%async_computation.4 | async-start | bytes 1572864 | tf_op jit(solution)/shard_map/psum | solution.py:84
  685.8 29.4 %slice-start.2 = ((s8[4718592]{0:T(1024)(128)(4,1)}), s8[4194304]{0:T(1024)(128)(4,1)S(1)}, s32[]{:S(2)}) async-start(s8[4718592]{0:T(1024)(128)(4,1)} %bitcast.110), calls=%async_computation.12 | async-start | bytes 8388608
  689.4 1.5 copy-start.15
  689.4 25.7 %slice-start.3 = ((s8[4718592]{0:T(1024)(128)(4,1)}), s8[524288]{0:T(1024)(128)(4,1)S(1)}, s32[]{:S(2)}) async-start(s8[4718592]{0:T(1024)(128)(4,1)} %bitcast.110), calls=%async_computation.13 | async-start | bytes 1048576
  689.4 20.3 %collective-permute-start.2 = (bf16[64,6144]{1,0:T(8,128)(2,1)S(1)}, bf16[64,6144]{1,0:T(8,128)(2,1)S(1)}, u32[]{:S(2)}, u32[]{:S(2)}) collective-permute-start(bf16[64,6144]{1,0:T(8,128)(2,1)S(1)} %fusion.52), channel_id=1, source_target_pairs={{128,0},{129,1},{130,2},{131,3},{132,4},{133,5},{134,6},{135,7},{1... | collective-permute-start | bytes 2359304 | tf_op jit(solution)/shard_map/ppermute | solution.py:12
  709.7 6.4 slice-start.10
  711.1 5.1 slice-start.11
  718.1 329.2 %all-reduce.15.cloned.1.call-start = ((), (), s32[]{:S(2)}) async-start(), calls=%async_computation.9 | async-start | bytes 3145728 | tf_op jit(solution)/shard_map/psum | solution.py:66
  863.6 5.8 copy-start.16
  863.6 20.1 %collective-permute-start.3 = (bf16[64,6144]{1,0:T(8,128)(2,1)S(1)}, bf16[64,6144]{1,0:T(8,128)(2,1)S(1)}, u32[]{:S(2)}, u32[]{:S(2)}) collective-permute-start(bf16[64,6144]{1,0:T(8,128)(2,1)S(1)} %fusion.55), channel_id=1, source_target_pairs={{128,0},{129,1},{130,2},{131,3},{132,4},{133,5},{134,6},{135,7},{1... | collective-permute-start | bytes 2359304 | tf_op jit(solution)/shard_map/ppermute | solution.py:12
  865.1 18.7 %copy-start.11 = (bf16[64,6144]{1,0:T(8,128)(2,1)S(1)}, bf16[64,6144]{1,0:T(8,128)(2,1)}, u32[]{:S(2)}) copy-start(bf16[64,6144]{1,0:T(8,128)(2,1)} %copy-done.10) | copy-start | bytes 2359300
  883.7 5.7 slice-start.16
  883.8 5.6 copy-start.9
  883.8 5.6 slice-start.17
  883.8 7.2 copy-start.1
  883.8 7.2 copy-start.3
  883.8 7.2 copy-start.5
  889.4 9.6 slice-start.4
  889.4 10.5 slice-start.12
  891.0 7.9 slice-start.5
  891.0 8.9 slice-start.13
  901.9 298.8 %reduce-scatter.2.cloned.1.call-start = ((), (), s32[]{:S(2)}) async-start(), calls=%async_computation.5 | async-start | bytes 15925248 | tf_op jit(solution)/shard_map/reduce_scatter | solution.py:104
  918.6 130.0 %copy-start.8 = (bf16[2,64,6144]{2,1,0:T(8,128)(2,1)S(1)}, bf16[2,64,6144]{2,1,0:T(8,128)(2,1)}, u32[]{:S(2)}) copy-start(bf16[2,64,6144]{2,1,0:T(8,128)(2,1)} %param.5) | copy-start | bytes 4718596
  1047.3 1.4 copy-start.12
Sparse Core Ops, SparseCore 0:
  9.8 63.5 all-gather.6
  75.2 58.3 all-gather.8
  135.3 58.3 all-gather.10
  198.1 142.9 all-reduce.6
  369.4 145.0 all-reduce.8
  540.7 145.0 all-reduce.10
  718.3 142.1 all-reduce.12
  902.0 145.2 all-reduce.14
  1050.1 150.5 reduce-scatter.1
where the time goes:
time: 1210 us
  waiting for transfers between devices  1090 us (90%)
  matrix products  58.9 us (5%)
  other arithmetic  38.8 us (3%)
  between operations  14.6 us (1%)
    psum x3, waiting for transfers between devices, shards(): lax.psum(jnp.dot(h, w_down, preferred_element_type=jnp.float32).astype(jn...  416 us
    psum x2, waiting for transfers between devices, shards(): lax.psum(partial_value.astype(jnp.bfloat16), 'tensor').astype(jnp.float32)  287 us
    reduce_scatter x1, waiting for transfers between devices, shards(): lax.psum_scatter((jnp.concatenate([first_part, second_part], axis=1) * sc...  149 us
    all_gather x1, waiting for transfers between devices, shards(): lax.all_gather(gate_weight[0], 'dp', axis=1, tiled=True)  61 us
    ppermute x4, waiting for transfers between devices, passed_along(): return lax.ppermute(block, axis, route)  57.8 us
    all_gather x1, waiting for transfers between devices, shards(): lax.all_gather(up_weight[0], 'dp', axis=1, tiled=True)  56.3 us
    all_gather x1, waiting for transfers between devices, shards(): lax.all_gather(down_weight[0], 'dp', axis=1, tiled=True)  56.3 us
  transfers between devices with their start and end apart: 13, of which 13 were waited for; matrix products, arithmetic and copies ran while one was open for 4% of the time, Pallas kernels for 0%

commit v1 on v0

v1 whole, which is shorter than its diff:
```python
import functools
import math

import jax
import jax.numpy as jnp
from jax import lax
from jax.experimental import pallas as pl
from jax.experimental.pallas import tpu as pltpu
from jax.sharding import PartitionSpec as P

MESH = pl.DeviceIdType.MESH
BF16 = jnp.bfloat16
F32 = jnp.float32
EPS = 1e-05
LANES = 128
LAG_FORWARD = 2
LAG_BACKWARD = 2
LAG_LATE = 1


def dot_nt(a, b):
    return lax.dot_general(a, b, (((1,), (1,)), ((), ())), preferred_element_type=F32)


def dot_tn(a, b):
    return lax.dot_general(a, b, (((0,), (0,)), ((), ())), preferred_element_type=F32)


def fold(block):
    half = block.shape[1] // 2
    return jnp.concatenate([block[:, :half], block[:, half:]], axis=0)


def unfold(block):
    half = block.shape[0] // 2
    return jnp.concatenate([block[:half], block[half:]], axis=1)


def hops(b):
    return (4, 3) if b % 2 == 0 else (3, 4)


def row_column(value, rows):
    high = value.astype(BF16).astype(F32)
    lane = lax.broadcasted_iota(jnp.int32, (rows, LANES), 1)
    return jnp.where(lane == 0, high, jnp.where(lane == 1, value - high, 0.0))


def kernel(
    sizes,
    feed, gate_hbm, up_hbm, down_hbm,
    out_ref, grad_ref, gg_ref, gu_ref, gd_ref,
    w_pair, w_down, feed_in, x_all, g_all,
    part_u, send_u, recv_u, part_v, send_v, recv_v,
    act, scale_r, h_all, d_all,
    core_src, core_dst, slab_src, slab_dst, row_src, fold_src, fold_dst,
    acc_pair, acc_down,
    w_sem, feed_s, feed_r, bcast_s, bcast_r, core_s, core_r,
    rsu_s, rsu_r, rsv_s, rsv_r, agh_s, agh_r, agd_s, agd_r,
    slab_s, slab_r, row_s, fold_s, fold_r,
):
    nb, dp, chips, rows, width, hid, tokens = sizes
    slabs = 2 * chips
    batch = slabs * rows
    chunk = batch // dp
    sec = lax.axis_index("section")
    d = lax.axis_index("dp")
    t = lax.axis_index("tensor")
    k = t // 2
    c = t % 2
    other = 1 - sec
    mine = c * chips + k
    pair = 2 * hid

    def at(**axes):
        return axes

    def turn(base, step, size):
        return lax.rem(base + step + size, size)

    def z_at(step):
        return at(dp=turn(d, step, dp))

    def chip_at(j):
        return at(tensor=turn(k, j, chips) * 2 + c)

    sibling = at(tensor=k * 2 + (1 - c))

    def rcopy(src, dst, ss, rs, dev):
        return pltpu.make_async_remote_copy(
            src_ref=src, dst_ref=dst, send_sem=ss, recv_sem=rs, device_id=dev, device_id_type=MESH
        )

    loads = [
        pltpu.make_async_copy(gate_hbm, w_pair.at[pl.ds(0, hid)], w_sem.at[0]),
        pltpu.make_async_copy(up_hbm, w_pair.at[pl.ds(hid, hid)], w_sem.at[1]),
        pltpu.make_async_copy(down_hbm, w_down, w_sem.at[2]),
    ]
    for load in loads:
        load.start()

    barrier = pltpu.get_barrier_semaphore()
    for j in range(1, dp):
        pl.semaphore_signal(barrier, inc=1, device_id=z_at(j), device_id_type=MESH)
    for j in range(1, chips):
        pl.semaphore_signal(barrier, inc=1, device_id=chip_at(j), device_id_type=MESH)
    for j in range(chips):
        pl.semaphore_signal(
            barrier, inc=1, device_id=at(section=other, **chip_at(j)), device_id_type=MESH
        )
    pl.semaphore_signal(barrier, inc=1, device_id=sibling, device_id_type=MESH)
    pl.semaphore_wait(barrier, dp - 1 + chips - 1 + chips + 1)

    ends = []

    def feed_all():
        for j in range(1, dp):
            to = turn(d, j, dp)
            rcopy(feed.at[to], feed_in.at[d], feed_s.at[0], feed_r.at[d], z_at(j)).start()
        ends.append(
            lambda: rcopy(
                feed_in.at[pl.ds(0, dp - 1)], feed_in.at[pl.ds(0, dp - 1)], feed_s.at[0], feed_r.at[0], z_at(1)
            ).wait_send()
        )
        feed_in[d] = feed[d]

    def feed_slab(way, into, b):
        halves = []
        for source in (2 * b, 2 * b + 1):

            @pl.when(d != source)
            def _():
                rcopy(feed.at[source], feed_in.at[source], feed_s.at[0], feed_r.at[source], z_at(1)).wait_recv()

        for source in (2 * b, 2 * b + 1):
            halves.append(unfold(feed_in[source].astype(F32)))
        into[b, mine] = jnp.concatenate(halves, axis=0).astype(BF16)
        for j in range(1, chips):
            rcopy(
                into.at[b, mine], into.at[b, mine], bcast_s.at[way, b], bcast_r.at[way, b], chip_at(j)
            ).start()
        seven = into.at[b, pl.ds(0, chips - 1)]
        ends.append(lambda: rcopy(seven, seven, bcast_s.at[way, b], bcast_r.at[way, b], z_at(1)).wait_send())

    def slabs_to_core(way, into, count, b):
        some = into.at[b, pl.ds(0, count)]
        rcopy(some, some, bcast_s.at[way, b], bcast_r.at[way, b], z_at(1)).wait_recv()
        own = into.at[b, pl.ds(c * chips, chips)]
        copy = rcopy(own, own, core_s.at[way, b], core_r.at[way, b], sibling)
        copy.start()
        ends.append(copy.wait_send)

    def wait_core(way, into, b):
        rest = into.at[b, pl.ds((1 - c) * chips, chips)]
        rcopy(rest, rest, core_s.at[way, b], core_r.at[way, b], sibling).wait_recv()

    def rs_step(step, part, src, dst, ss, rs, b):
        for way, count in enumerate(hops(b)):
            if step > count:
                continue
            sign = 1 - 2 * way
            at_chunk = turn(d, sign * (count + 1 - step), dp)
            value = part[b, at_chunk]
            if step > 1:
                rcopy(
                    src.at[b, way, step - 2], dst.at[b, way, step - 2], ss.at[b, way, step - 2],
                    rs.at[b, way, step - 2], z_at(sign),
                ).wait_recv()
                value = value + dst[b, way, step - 2].astype(F32)
            src[b, way, step - 1] = value.astype(BF16)
            copy = rcopy(
                src.at[b, way, step - 1], dst.at[b, way, step - 1], ss.at[b, way, step - 1],
                rs.at[b, way, step - 1], z_at(sign),
            )
            copy.start()
            ends.append(copy.wait_send)

    def rs_total(part, src, dst, ss, rs, b):
        total = part[b, d]
        for way, count in enumerate(hops(b)):
            sign = 1 - 2 * way
            rcopy(
                src.at[b, way, count - 1], dst.at[b, way, count - 1], ss.at[b, way, count - 1],
                rs.at[b, way, count - 1], z_at(sign),
            ).wait_recv()
            total = total + dst[b, way, count - 1].astype(F32)
        return total

    def ag_wait(step, buf, ss, rs, way, b):
        sign = 1 - 2 * way
        got = buf.at[b, turn(d, -sign * step, dp)]
        rcopy(got, got, ss.at[b, way, step - 1], rs.at[b, way, step - 1], z_at(sign)).wait_recv()

    def ag_step(step, buf, ss, rs, b):
        for way, count in enumerate(hops(b)):
            if step > count:
                continue
            sign = 1 - 2 * way
            if step > 1:
                ag_wait(step - 1, buf, ss, rs, way, b)
            piece = buf.at[b, turn(d, -sign * (step - 1), dp)]
            copy = rcopy(piece, piece, ss.at[b, way, step - 1], rs.at[b, way, step - 1], z_at(sign))
            copy.start()
            ends.append(copy.wait_send)

    def ag_finish(buf, ss, rs, b):
        for way, count in enumerate(hops(b)):
            ag_wait(count, buf, ss, rs, way, b)

    rs_u = (part_u, send_u, recv_u, rsu_s, rsu_r)
    rs_v = (part_v, send_v, recv_v, rsv_s, rsv_r)
    ag_h = (h_all, agh_s, agh_r)
    ag_d = (d_all, agd_s, agd_r)

    def project_up(b):
        wait_core(0, x_all, b)
        x = x_all[b].reshape(batch, width)
        u = dot_nt(x, w_pair[...])
        xf = x.astype(F32)
        squares = jnp.sum(xf * xf, axis=1, keepdims=True)
        part_u[b, :, :, 0:pair] = u.reshape(dp, chunk, pair)
        part_u[b, :, :, pair:] = row_column(squares, batch).reshape(dp, chunk, LANES)
        rs_step(1, *rs_u, b)

    def project_dh(b):
        wait_core(1, g_all, b)
        g = g_all[b].reshape(batch, width)
        part_v[b] = dot_nt(g, w_down[...]).reshape(dp, chunk, hid)
        rs_step(1, *rs_v, b)

    def hidden(send, b):
        total = rs_total(*rs_u, b)
        squares = jnp.sum(total[:, pair:], axis=1, keepdims=True)
        r = lax.rsqrt(squares / (width * dp) + EPS)
        ab = total[:, :pair] * r
        a, up = ab[:, :hid], ab[:, hid:]
        act[b] = ab
        scale_r[b] = jnp.broadcast_to(r, (chunk, LANES))
        h_all[b, d] = (a * jax.nn.sigmoid(a) * up).astype(BF16)
        if send:
            ag_step(1, *ag_h, b)

    def hidden_grad(b):
        dh = rs_total(*rs_v, b)
        r = scale_r[b][:, 0:1]
        a, up = act[b, :, :hid], act[b, :, hid:]
        sig = jax.nn.sigmoid(a)
        da = (r * (dh * up * sig * (1.0 + a * (1.0 - sig)))).astype(BF16)
        db = (r * (dh * a * sig)).astype(BF16)
        mixed = r * jnp.sum(da.astype(F32) * a + db.astype(F32) * up, axis=1, keepdims=True)
        d_all[b, d, :, 0:hid] = da
        d_all[b, d, :, hid:pair] = db
        d_all[b, d, :, pair:] = row_column(mixed, chunk).astype(BF16)
        ag_step(1, *ag_d, b)

    def to_sibling(way, b):
        rest = core_src.at[way, b, pl.ds((1 - c) * chips, chips)]
        copy = rcopy(rest, core_dst.at[way, b], core_s.at[2 + way, b], core_r.at[2 + way, b], sibling)
        copy.start()
        ends.append(copy.wait_send)

    def project_down(b):
        ag_finish(*ag_h, b)
        h = h_all[b].reshape(batch, hid)
        p = jnp.dot(h, w_down[...], preferred_element_type=F32)
        core_src[0, b] = p.astype(BF16).reshape(slabs, rows, width)
        to_sibling(0, b)

    def project_dn(b):
        ag_finish(*ag_d, b)
        flat = d_all[b].reshape(batch, pair + LANES)
        mixed = jnp.sum(flat[:, pair:].astype(F32), axis=1, keepdims=True)
        q = jnp.dot(flat[:, :pair], w_pair[...], preferred_element_type=F32)
        xf = x_all[b].reshape(batch, width).astype(F32)
        q = q - xf * (mixed * (1.0 / (width * dp)))
        core_src[1, b] = q.astype(BF16).reshape(slabs, rows, width)
        to_sibling(1, b)

    def scatter_slabs(way, b):
        rest = core_dst.at[way, b]
        rcopy(rest, rest, core_s.at[2 + way, b], core_r.at[2 + way, b], sibling).wait_recv()
        both = core_src[way, b, pl.ds(c * chips, chips)].astype(F32) + core_dst[way, b].astype(F32)
        slab_src[way, b] = both.astype(BF16)
        for j in range(1, chips):
            to = turn(k, j, chips)
            rcopy(
                slab_src.at[way, b, to], slab_dst.at[way, b, k], slab_s.at[way, b], slab_r.at[way, b], chip_at(j)
            ).start()
        seven = slab_dst.at[way, b, pl.ds(0, chips - 1)]
        ends.append(lambda: rcopy(seven, seven, slab_s.at[way, b], slab_r.at[way, b], z_at(1)).wait_send())

    def slab_total(way, b):
        seven = slab_dst.at[way, b, pl.ds(0, chips - 1)]
        rcopy(seven, seven, slab_s.at[way, b], slab_r.at[way, b], z_at(1)).wait_recv()
        total = slab_src[way, b, k].astype(F32)
        for j in range(1, chips):
            total = total + slab_dst[way, b, turn(k, j, chips)].astype(F32)
        return total

    def finish_slab(way, value, into, b):
        row_src[way, b] = value.astype(BF16)
        if into is not None:
            for j in range(chips):
                rcopy(
                    row_src.at[way, b], into.at[b, mine], row_s.at[way, b], bcast_r.at[way, b],
                    at(section=other, **chip_at(j)),
                ).start()
            eight = into.at[b, pl.ds(0, chips)]
            ends.append(lambda: rcopy(eight, eight, row_s.at[way, b], bcast_r.at[way, b], z_at(1)).wait_send())
        value = value.astype(BF16).astype(F32)
        half = rows // 2
        for i in range(2):
            owner = 2 * b + i
            fold_src[way, b, i] = fold(value[i * half : (i + 1) * half]).astype(BF16)
            copy = rcopy(
                fold_src.at[way, b, i], fold_dst.at[way, d], fold_s.at[way, b, i], fold_r.at[way], at(dp=owner)
            )

            @pl.when(d == owner)
            def _():
                fold_dst[way, d] = fold_src[way, b, i]

            @pl.when(d != owner)
            def _():
                copy.start()

            def end(copy=copy, owner=owner):
                @pl.when(d != owner)
                def _():
                    copy.wait_send()

            ends.append(end)

    def finish_out(into, b):
        finish_slab(0, x_all[b, mine].astype(F32) + slab_total(0, b), into, b)

    def finish_grad(into, b):
        finish_slab(1, g_all[b, mine].astype(F32) + slab_total(1, b), into, b)

    def weight_grads(b):
        x = x_all[b].reshape(batch, width)
        g = g_all[b].reshape(batch, width)
        pair_part = dot_tn(d_all[b].reshape(batch, pair + LANES)[:, :pair], x)
        down_part = dot_tn(h_all[b].reshape(batch, hid), g)
        if b == 0:
            acc_pair[...] = pair_part
            acc_down[...] = down_part
        else:
            acc_pair[...] += pair_part
            acc_down[...] += down_part

    def collect(way, ref):
        seven = fold_dst.at[way, pl.ds(0, dp - 1)]
        rcopy(seven, seven, fold_s.at[way, 0, 0], fold_r.at[way], z_at(1)).wait_recv()
        for source in range(dp):
            ref[:, source * width : (source + 1) * width] = unfold(fold_dst[way, source].astype(F32))

    def wave(ops, lag):
        for tick in range(len(ops) + lag * (nb - 1)):
            for b in range(nb):
                index = tick - lag * b
                if 0 <= index < len(ops):
                    ops[index](b)

    def part(function, *args):
        return functools.partial(function, *args)

    def rs_ops(which):
        return [part(rs_step, step, *which) for step in (2, 3, 4)]

    def ag_ops(which):
        return [part(ag_step, step, *which) for step in (2, 3, 4)]

    def both(*functions):
        def run(b):
            for function in functions:
                function(b)

        return run

    def wait_weights():
        for load in loads:
            load.wait()

    def close():
        scale = 1.0 / math.sqrt(tokens)
        gg_ref[...] = (acc_pair[0:hid] * scale).astype(BF16)
        gu_ref[...] = (acc_pair[hid:pair] * scale).astype(BF16)
        gd_ref[...] = (acc_down[...] * scale).astype(BF16)
        collect(0, out_ref)
        collect(1, grad_ref)
        for end in ends:
            end()
        ends.clear()

    feed_all()
    shared = list(ends)

    @pl.when(sec == 0)
    def _():
        ends[:] = shared
        wait_weights()
        wave(
            [
                part(feed_slab, 0, x_all),
                part(slabs_to_core, 0, x_all, chips - 1),
                project_up,
                *rs_ops(rs_u),
                part(hidden, True),
                *ag_ops(ag_h),
                project_down,
                part(scatter_slabs, 0),
                part(finish_out, x_all),
            ],
            LAG_FORWARD,
        )
        wave(
            [
                part(slabs_to_core, 1, g_all, chips),
                project_dh,
                *rs_ops(rs_v),
                hidden_grad,
                *ag_ops(ag_d),
                project_dn,
                part(scatter_slabs, 1),
                both(weight_grads, part(finish_grad, None)),
            ],
            LAG_BACKWARD,
        )
        close()

    @pl.when(sec == 1)
    def _():
        ends[:] = shared
        wait_weights()
        wave(
            [
                part(feed_slab, 1, g_all),
                part(slabs_to_core, 1, g_all, chips - 1),
                project_dh,
                *rs_ops(rs_v),
            ],
            1,
        )
        wave(
            [
                part(slabs_to_core, 0, x_all, chips),
                project_up,
                *rs_ops(rs_u),
                both(part(hidden, False), hidden_grad),
                *ag_ops(ag_d),
                project_dn,
                part(scatter_slabs, 1),
                part(finish_grad, g_all),
            ],
            LAG_BACKWARD,
        )
        wave(
            [
                part(ag_step, 1, *ag_h),
                *ag_ops(ag_h),
                project_down,
                part(scatter_slabs, 0),
                both(weight_grads, part(finish_out, None)),
            ],
            LAG_LATE,
        )
        close()


def shards(inputs, cotangent, gate_weight, up_weight, down_weight):
    first = lax.axis_index("section") == 0
    dp, tensors = lax.axis_size("dp"), lax.axis_size("tensor")
    micro, tok_dev, model = inputs.shape
    _, hid, width = gate_weight.shape
    chips = tensors // 2
    share = tok_dev // tensors
    held = micro * share
    nb, rows = dp // 2, 2 * held
    batch = tensors * rows
    chunk = batch // dp
    pair = 2 * hid
    start = lax.axis_index("tensor") * share
    pick = jnp.where(
        first,
        lax.dynamic_slice_in_dim(inputs, start, share, 1),
        lax.dynamic_slice_in_dim(cotangent, start, share, 1),
    )
    feed = pick.reshape(held, dp, 2, width // 2).transpose(1, 2, 0, 3).reshape(dp, rows, width // 2)

    def sems(*shape):
        return pltpu.SemaphoreType.DMA(shape)

    def bf16(*shape):
        return pltpu.VMEM(shape, BF16)

    def f32(*shape):
        return pltpu.VMEM(shape, F32)

    sizes = (nb, dp, chips, rows, width, hid, micro * tok_dev * dp)
    vmem = pl.BlockSpec(memory_space=pltpu.VMEM)
    anywhere = pl.BlockSpec(memory_space=pl.ANY)
    out, grad, grad_gate, grad_up, grad_down = pl.pallas_call(
        functools.partial(kernel, sizes),
        out_shape=[
            jax.ShapeDtypeStruct((held, model), F32),
            jax.ShapeDtypeStruct((held, model), F32),
            jax.ShapeDtypeStruct((hid, width), BF16),
            jax.ShapeDtypeStruct((hid, width), BF16),
            jax.ShapeDtypeStruct((hid, width), BF16),
        ],
        in_specs=[vmem, anywhere, anywhere, anywhere],
        out_specs=[vmem] * 5,
        scratch_shapes=[
            bf16(pair, width),
            bf16(hid, width),
            bf16(dp, rows, width // 2),
            bf16(nb, tensors, rows, width),
            bf16(nb, tensors, rows, width),
            f32(nb, dp, chunk, pair + LANES),
            bf16(nb, 2, 4, chunk, pair + LANES),
            bf16(nb, 2, 4, chunk, pair + LANES),
            f32(nb, dp, chunk, hid),
            bf16(nb, 2, 4, chunk, hid),
            bf16(nb, 2, 4, chunk, hid),
            f32(nb, chunk, pair),
            f32(nb, chunk, LANES),
            bf16(nb, dp, chunk, hid),
            bf16(nb, dp, chunk, pair + LANES),
            bf16(2, nb, tensors, rows, width),
            bf16(2, nb, chips, rows, width),
            bf16(2, nb, chips, rows, width),
            bf16(2, nb, chips, rows, width),
            bf16(2, nb, rows, width),
            bf16(2, nb, 2, rows, width // 2),
            bf16(2, dp, rows, width // 2),
            f32(pair, width),
            f32(hid, width),
            sems(3),
            sems(1),
            sems(dp),
            sems(2, nb),
            sems(2, nb),
            sems(4, nb),
            sems(4, nb),
            *[sems(nb, 2, 4) for _ in range(8)],
            sems(2, nb),
            sems(2, nb),
            sems(2, nb),
            sems(2, nb, 2),
            sems(2),
        ],
        compiler_params=pltpu.CompilerParams(
            collective_id=0, has_side_effects=True, vmem_limit_bytes=56 * 1024 * 1024
        ),
    )(feed, gate_weight[0], up_weight[0], down_weight[0])
    section_out = out.astype(BF16).reshape(1, micro, share, model)
    section_grad = grad.astype(BF16).reshape(1, micro, share, model)
    return (section_out, section_grad, grad_gate[None], grad_up[None], grad_down[None])


def solution(mesh):
    in_specs = (
        P(None, "dp", None),
        P(None, "dp", None),
        P("section", "tensor", "dp"),
        P("section", "tensor", "dp"),
        P("section", "tensor", "dp"),
    )
    out_specs = (
        P("section", None, ("dp", "tensor"), None),
        P("section", None, ("dp", "tensor"), None),
        P("section", "tensor", "dp"),
        P("section", "tensor", "dp"),
        P("section", "tensor", "dp"),
    )
    return jax.shard_map(shards, mesh=mesh, in_specs=in_specs, out_specs=out_specs, check_vma=False)
```

time: 1210 us -> 195 us (0.16)
  waiting for transfers between devices: 1090 us -> 0 us
  Pallas kernels: 0 us -> 185 us
  matrix products: 58.9 us -> 0 us
  other arithmetic: 38.8 us -> 3.07 us
  between operations: 14.6 us -> 0.68 us
    psum x5 -> x0, waiting for transfers between devices: 703 us -> none  [the longest x3 416 us: shards(): lax.psum(jnp.dot(h, w_down, preferred_element_type=jnp.float32).astype(jn...]
    pallas_call x0 -> x1, Pallas kernels: none -> 185 us  [shards(): pl.pallas_call(functools.partial(kernel, sizes), out_shape=[jax.ShapeDtyp...]
    all_gather x3 -> x0, waiting for transfers between devices: 174 us -> none  [the longest x1 61 us: shards(): lax.all_gather(gate_weight[0], 'dp', axis=1, tiled=True)]
    reduce_scatter x1 -> x0, waiting for transfers between devices: 149 us -> none  [shards(): lax.psum_scatter((jnp.concatenate([first_part, second_part], axis=1) * sc...]
    dot_general x20 -> x0, matrix products: 58.9 us -> none  [the longest x3 10.4 us: shards(): jnp.dot(h, w_down, preferred_element_type=jnp.float32).astype(jnp.bfloat16)]
    ppermute x4 -> x0, waiting for transfers between devices: 57.8 us -> none  [passed_along(): return lax.ppermute(block, axis, route)]
    convert_element_type x9 -> x2, other arithmetic: 26.1 us -> 1.94 us  [the longest x1 1 us: shards(): section_out = out.astype(BF16).reshape(1, micro, share, model)]
  transfers between devices with their start and end apart: 13 -> 0, of which waited for: 13 -> 0; matrix products, arithmetic and copies ran while one was open for 4% -> 0% of each run, Pallas kernels for 0% -> 0%
where the time goes in v1:
time: 195 us
  Pallas kernels  185 us (95%)
  local copies, waits for them, and re-layouts  5.65 us (3%)
  other arithmetic  3.07 us (2%)
    pallas_call x1, Pallas kernels, shards(): pl.pallas_call(functools.partial(kernel, sizes), out_shape=[jax.ShapeDtyp...  185 us

profile of v1, /device:TPU:1, one launch (start us, length us, event | category | flops | bytes accessed | tf_op | source)
XLA Modules:
  0.0 194.5 jit_solution(14252393184591137023)
XLA Ops:
  0.6 1.1 dynamic-slice_select_fusion
  1.8 0.1 reshape.22
  1.8 0.7 copy.12
  2.5 185.1 %shard_map.92 = (f32[8,6144]{1,0:T(8,128)}, f32[8,6144]{1,0:T(8,128)}, bf16[384,768]{1,0:T(8,128)(2,1)}, bf16[384,768]{1,0:T(8,128)(2,1)}, bf16[384,768]{1,0:T(8,128)(2,1)}) custom-call(bf16[8,16,384]{2,1,0:T(8,128)(2,1)} %bitcast.17, bf16[384,768]{1,0:T(8,128)(2,1)} %bitcast.11, bf16[384,768]{1,0:T(8,128)(2,1)} %bitcast.12, bf16[384,768]{1,0:T(8,128)(2,1)} %bitcast.13), custom_call_target="tpu_custom_call" | custom-call | tf_op jit(solution)/shard_map/pallas_call | solution.py:503
  187.7 0.0 copy-start.1
  187.7 1.0 convert_element_type.6
  188.7 0.0 copy-start
  188.7 0.7 reshape.24
  189.4 0.9 convert_element_type.7
  190.3 0.7 reshape.25
  191.0 1.9 copy.16
  192.9 0.0 copy-done.1
  192.9 0.8 copy.17
  193.7 0.0 copy-done
  193.7 0.8 copy.18
Async XLA Ops:
  187.7 5.2 %copy-start.1 = (bf16[384,768]{1,0:T(8,128)(2,1)S(1)}, bf16[384,768]{1,0:T(8,128)(2,1)}, u32[]{:S(2)}) copy-start(bf16[384,768]{1,0:T(8,128)(2,1)} %get-tuple-element.13) | copy-start | bytes 1769476
  188.7 5.1 %copy-start = (bf16[384,768]{1,0:T(8,128)(2,1)S(1)}, bf16[384,768]{1,0:T(8,128)(2,1)}, u32[]{:S(2)}) copy-start(bf16[384,768]{1,0:T(8,128)(2,1)} %get-tuple-element.14) | copy-start | bytes 1769476

commit v2 on v1

v2 whole, which is shorter than its diff:
```python
import functools
import math

import jax
import jax.numpy as jnp
from jax import lax
from jax.experimental import pallas as pl
from jax.experimental.pallas import tpu as pltpu
from jax.sharding import PartitionSpec as P

MESH = pl.DeviceIdType.MESH
BF16 = jnp.bfloat16
F32 = jnp.float32
EPS = 1e-05
LANES = 128
ORDER_FIRST = (
    (0, 0), (0, 1), (0, 2), (0, 3), (0, 4), (0, 5), (0, 6), (0, 7), (1, 0), (1, 1), (2, 0), (2, 1), (1, 2), (1, 3), (2, 2),
    (2, 3), (1, 4), (3, 0), (1, 5), (3, 1), (2, 4), (1, 6), (2, 5), (2, 6), (3, 2), (1, 7), (3, 3), (2, 7), (4, 0), (4, 1),
    (3, 4), (3, 5), (3, 6), (4, 2), (4, 3), (3, 7), (5, 0), (5, 1), (4, 4), (4, 5), (4, 6), (5, 3), (5, 2), (4, 7), (6, 0),
    (6, 1), (5, 4), (5, 6), (5, 5), (5, 7), (6, 2), (6, 3), (6, 5), (11, 0), (12, 0), (6, 4), (6, 7), (6, 6), (11, 1), (12, 1),
    (11, 2), (12, 2), (13, 0), (11, 3), (12, 3), (13, 1), (11, 5), (12, 5), (13, 2), (11, 4), (12, 4), (11, 7), (13, 3),
    (12, 7), (13, 5), (11, 6), (12, 6), (13, 4), (13, 7), (13, 6), (14, 1), (15, 1), (14, 0), (15, 0), (16, 1), (14, 2),
    (16, 0), (15, 2), (14, 3), (19, 1), (15, 3), (14, 5), (19, 0), (16, 2), (14, 7), (15, 5), (15, 7), (14, 4), (20, 1),
    (15, 4), (16, 3), (20, 0), (14, 6), (19, 2), (15, 6), (16, 5), (16, 7), (21, 1), (16, 4), (19, 3), (21, 0), (20, 2),
    (16, 6), (19, 5), (22, 1), (19, 7), (20, 3), (19, 4), (22, 0), (21, 2), (19, 6), (23, 1), (20, 5), (20, 7), (24, 1),
    (20, 4), (21, 3), (23, 0), (26, 0), (26, 1), (22, 2), (24, 0), (20, 6), (21, 5), (21, 7), (21, 4), (22, 3), (25, 1),
    (21, 6), (23, 2), (22, 5), (26, 2), (22, 7), (22, 4), (25, 0), (24, 2), (23, 3), (26, 3), (22, 6), (24, 3), (23, 5),
    (23, 7), (23, 4), (24, 5), (24, 7), (26, 4), (26, 5), (23, 6), (24, 4), (25, 2), (26, 6), (24, 6), (26, 7), (25, 3),
    (25, 5), (25, 4), (25, 7), (25, 6),
)
ORDER_SECOND = (
    (0, 1), (0, 0), (0, 2), (0, 3), (0, 4), (0, 5), (0, 6), (0, 7), (14, 0), (15, 0), (14, 1), (15, 1), (14, 2), (14, 4),
    (14, 3), (15, 2), (15, 3), (14, 5), (15, 4), (16, 0), (14, 7), (15, 5), (16, 1), (14, 6), (15, 6), (16, 2), (16, 3),
    (15, 7), (16, 4), (16, 6), (16, 5), (1, 0), (16, 7), (2, 0), (1, 1), (2, 1), (1, 2), (3, 0), (2, 2), (3, 1), (1, 3),
    (2, 3), (4, 0), (3, 2), (1, 5), (4, 1), (2, 5), (1, 4), (3, 3), (5, 0), (2, 4), (1, 7), (4, 2), (5, 1), (2, 7), (3, 5),
    (1, 6), (4, 3), (6, 0), (19, 0), (2, 6), (3, 4), (6, 1), (19, 1), (5, 2), (3, 7), (4, 5), (5, 3), (20, 0), (3, 6), (4, 4),
    (20, 1), (6, 2), (19, 2), (4, 7), (5, 5), (21, 0), (6, 3), (19, 3), (4, 6), (5, 4), (21, 1), (5, 7), (20, 2), (6, 5),
    (19, 5), (20, 3), (5, 6), (22, 0), (22, 1), (6, 4), (19, 4), (6, 7), (19, 7), (21, 2), (20, 5), (21, 3), (6, 6), (19, 6),
    (23, 1), (20, 4), (23, 0), (20, 7), (24, 1), (24, 0), (22, 2), (21, 5), (22, 3), (20, 6), (21, 4), (21, 7), (23, 2),
    (22, 5), (25, 1), (24, 2), (21, 6), (23, 3), (25, 0), (22, 4), (22, 7), (24, 3), (23, 5), (22, 6), (24, 5), (23, 4),
    (23, 7), (25, 2), (7, 0), (7, 1), (7, 2), (7, 3), (7, 4), (24, 7), (7, 5), (7, 7), (7, 6), (24, 4), (23, 6), (25, 3),
    (24, 6), (25, 5), (8, 0), (8, 1), (8, 2), (8, 4), (8, 3), (8, 5), (25, 7), (8, 6), (8, 7), (9, 0), (9, 1), (9, 2), (25, 4),
    (9, 4), (9, 3), (9, 5), (9, 6), (9, 7), (25, 6), (10, 1), (10, 0), (10, 2), (10, 4), (10, 7), (10, 5), (10, 3), (10, 6),
    (11, 1), (11, 2), (26, 2), (11, 0), (26, 0), (26, 1), (12, 0), (12, 1), (12, 2), (11, 3), (26, 3), (12, 3), (11, 4),
    (26, 4), (11, 5), (26, 5), (12, 4), (12, 5), (11, 6), (12, 6), (26, 6), (13, 4), (11, 7), (26, 7), (13, 0), (12, 7),
    (13, 1), (13, 2), (13, 3), (13, 5), (13, 6), (13, 7),
)


def dot_nt(a, b):
    return lax.dot_general(a, b, (((1,), (1,)), ((), ())), preferred_element_type=F32)


def dot_tn(a, b):
    return lax.dot_general(a, b, (((0,), (0,)), ((), ())), preferred_element_type=F32)


RING, PAIRS, DIRECT = 0, 1, 2
PARENT = ((0, 1, 2, 3), (0, 0, 2, 2), (0, 0, 0, 0))
ROUTES_FIRST = {
    "u": (RING,) * 8,
    "h": (DIRECT,) * 8,
    "v": (PAIRS,) * 8,
    "d": (RING,) * 8,
}
ROUTES_SECOND = {
    "u": (RING,) * 8,
    "h": (RING,) * 8,
    "v": (PAIRS,) * 8,
    "d": (RING,) * 8,
}


def hops(b):
    return (4, 3) if b % 2 == 0 else (3, 4)


def legs(kind, b, stage):
    pairs = []
    for way, count in enumerate(hops(b)):
        if kind == RING:
            some = [count + 1 - stage]
        elif kind == PAIRS:
            some = [(3, 4, 1), (2,)][stage - 1]
        else:
            some = (3, 4, 2, 1)
        pairs += [(way, s) for s in some if 1 <= s <= count]
    return pairs


def children(kind, count, s):
    return [later for later in range(s + 1, count + 1) if PARENT[kind][later - 1] == s]


def waited(kind, s):
    return (kind == RING and s <= 3) or (kind == PAIRS and s == 2)


def row_column(value, rows):
    high = value.astype(BF16).astype(F32)
    lane = lax.broadcasted_iota(jnp.int32, (rows, LANES), 1)
    return jnp.where(lane == 0, high, jnp.where(lane == 1, value - high, 0.0))


def kernel(
    sizes,
    feed, gate_hbm, up_hbm, down_hbm,
    out_ref, grad_ref, gg_ref, gu_ref, gd_ref,
    w_pair, w_down, x_all, g_all,
    part_u, send_u, recv_u, part_v, send_v, recv_v,
    act, scale_r, h_all, d_all,
    core_src, core_dst, slab_src, slab_dst, row_src, out_dst,
    acc_pair, acc_down,
    w_sem, feed_s, feed_r, bcast_s, bcast_r, core_s, core_r,
    rsu_s, rsu_r, rsv_s, rsv_r, agh_s, agh_r, agd_s, agd_r,
    slab_s, slab_r, row_s, out_s, out_r,
):
    nb, dp, chips, rows, width, hid, tokens = sizes
    half = width // 2
    batch = chips * rows
    chunk = batch // dp
    sec = lax.axis_index("section")
    d = lax.axis_index("dp")
    t = lax.axis_index("tensor")
    k = t // 2
    c = t % 2
    other = 1 - sec
    pair = 2 * hid

    def at(**axes):
        return axes

    def turn(base, step, size):
        return lax.rem(base + step + size, size)

    def z_at(step):
        return at(dp=turn(d, step, dp))

    def chip_at(j):
        return at(tensor=turn(k, j, chips) * 2 + c)

    sibling = at(tensor=k * 2 + (1 - c))

    def rcopy(src, dst, ss, rs, dev):
        return pltpu.make_async_remote_copy(
            src_ref=src, dst_ref=dst, send_sem=ss, recv_sem=rs, device_id=dev, device_id_type=MESH
        )

    loads = [
        pltpu.make_async_copy(gate_hbm, w_pair.at[pl.ds(0, hid)], w_sem.at[0]),
        pltpu.make_async_copy(up_hbm, w_pair.at[pl.ds(hid, hid)], w_sem.at[1]),
        pltpu.make_async_copy(down_hbm, w_down, w_sem.at[2]),
    ]
    for load in loads:
        load.start()

    barrier = pltpu.get_barrier_semaphore()
    for j in range(1, dp):
        pl.semaphore_signal(barrier, inc=1, device_id=z_at(j), device_id_type=MESH)
    for j in range(1, chips):
        pl.semaphore_signal(barrier, inc=1, device_id=chip_at(j), device_id_type=MESH)
    for j in range(chips):
        pl.semaphore_signal(
            barrier, inc=1, device_id=at(section=other, **chip_at(j)), device_id_type=MESH
        )
    for j in range(dp):
        pl.semaphore_signal(barrier, inc=1, device_id={**z_at(j), **sibling}, device_id_type=MESH)
    pl.semaphore_wait(barrier, dp - 1 + chips - 1 + chips + dp)

    ends = []

    def feed_all(into):
        for j in range(1, dp):
            rcopy(
                feed.at[turn(d, j, dp)], into.at[d, c, k], feed_s.at[0], feed_r.at[d], z_at(j)
            ).start()
        seven = feed.at[pl.ds(0, dp - 1)]
        ends.append(lambda: rcopy(seven, seven, feed_s.at[0], feed_r.at[0], z_at(1)).wait_send())
        into[d, c, k] = feed[d]

    def feed_slab(way, into, b):
        @pl.when(d != b)
        def _():
            rcopy(into.at[b, c, k], into.at[b, c, k], feed_s.at[0], feed_r.at[b], z_at(1)).wait_recv()

        for j in range(1, chips):
            rcopy(
                into.at[b, c, k], into.at[b, c, k], bcast_s.at[way, b], bcast_r.at[way, b], chip_at(j)
            ).start()
        seven = into.at[b, c, pl.ds(0, chips - 1)]
        ends.append(lambda: rcopy(seven, seven, bcast_s.at[way, b], bcast_r.at[way, b], z_at(1)).wait_send())

    def slabs_to_core(way, into, count, b):
        some = into.at[b, c, pl.ds(0, count)]
        rcopy(some, some, bcast_s.at[way, b], bcast_r.at[way, b], z_at(1)).wait_recv()
        own = into.at[b, c]
        copy = rcopy(own, own, core_s.at[way, b], core_r.at[way, b], sibling)
        copy.start()
        ends.append(copy.wait_send)

    def wait_core(way, into, b):
        rest = into.at[b, 1 - c]
        rcopy(rest, rest, core_s.at[way, b], core_r.at[way, b], sibling).wait_recv()

    def rs_copy(kind, way, s, src, dst, ss, rs, b):
        hop = (1 - 2 * way) * (s - PARENT[kind][s - 1])
        at_leg = (b, way, s - 1)
        return rcopy(src.at[at_leg], dst.at[at_leg], ss.at[at_leg], rs.at[at_leg], z_at(hop))

    def rs_step(stage, which, part, src, dst, ss, rs, b):
        kind = which[b]
        for way, s in legs(kind, b, stage):
            value = part[b, turn(d, (1 - 2 * way) * s, dp)]
            for later in children(kind, hops(b)[way], s):
                rs_copy(kind, way, later, src, dst, ss, rs, b).wait_recv()
                value = value + dst[b, way, later - 1].astype(F32)
            src[b, way, s - 1] = value.astype(BF16)
            copy = rs_copy(kind, way, s, src, dst, ss, rs, b)
            copy.start()
            ends.append(copy.wait_send)

    def rs_total(which, part, src, dst, ss, rs, b):
        kind = which[b]
        total = part[b, d]
        for way, count in enumerate(hops(b)):
            for s in children(kind, count, 0):
                rs_copy(kind, way, s, src, dst, ss, rs, b).wait_recv()
                total = total + dst[b, way, s - 1].astype(F32)
        return total

    def ag_copy(kind, way, s, buf, ss, rs, b, held):
        sign = 1 - 2 * way
        piece = buf.at[b, turn(d, -sign * held, dp)]
        return rcopy(
            piece, piece, ss.at[b, way, s - 1], rs.at[b, way, s - 1], z_at(sign * (s - PARENT[kind][s - 1]))
        )

    def ag_step(stage, which, buf, ss, rs, b):
        kind = which[b]
        held = 2 if kind == PAIRS and stage == 2 else stage - 1
        order = (3, 4, 2, 1) if held == 0 else (4, 3, 2, 1)
        for way, count in enumerate(hops(b)):
            if held:
                ag_copy(kind, way, held, buf, ss, rs, b, held).wait_recv()
            later = children(kind, count, held)
            for s in order:
                if s in later:
                    copy = ag_copy(kind, way, s, buf, ss, rs, b, held)
                    copy.start()
                    ends.append(copy.wait_send)

    def ag_finish(which, buf, ss, rs, b):
        kind = which[b]
        for way, count in enumerate(hops(b)):
            for s in range(1, count + 1):
                if not waited(kind, s):
                    ag_copy(kind, way, s, buf, ss, rs, b, s).wait_recv()

    routes = {}

    def rs_u():
        return (routes["u"], part_u, send_u, recv_u, rsu_s, rsu_r)

    def rs_v():
        return (routes["v"], part_v, send_v, recv_v, rsv_s, rsv_r)

    def ag_h():
        return (routes["h"], h_all, agh_s, agh_r)

    def ag_d():
        return (routes["d"], d_all, agd_s, agd_r)

    def whole(ref, b, count=1):
        parts = [ref[b : b + count, i].reshape(count * batch, half) for i in range(2)]
        return jnp.concatenate(parts, axis=1)

    def project_up(b):
        wait_core(0, x_all, b)
        x = whole(x_all, b)
        u = dot_nt(x, w_pair[...])
        xf = x.astype(F32)
        squares = jnp.sum(xf * xf, axis=1, keepdims=True)
        part_u[b, :, :, 0:pair] = u.reshape(dp, chunk, pair)
        part_u[b, :, :, pair:] = row_column(squares, batch).reshape(dp, chunk, LANES)
        rs_step(1, *rs_u(), b)

    def project_dh(b):
        wait_core(1, g_all, b)
        g = whole(g_all, b)
        part_v[b] = dot_nt(g, w_down[...]).reshape(dp, chunk, hid)
        rs_step(1, *rs_v(), b)

    def hidden(send, b):
        total = rs_total(*rs_u(), b)
        squares = jnp.sum(total[:, pair:], axis=1, keepdims=True)
        r = lax.rsqrt(squares / (width * dp) + EPS)
        ab = total[:, :pair] * r
        a, up = ab[:, :hid], ab[:, hid:]
        act[b] = ab
        scale_r[b] = jnp.broadcast_to(r, (chunk, LANES))
        h_all[b, d] = (a * jax.nn.sigmoid(a) * up).astype(BF16)
        if send:
            ag_step(1, *ag_h(), b)

    def hidden_grad(b):
        dh = rs_total(*rs_v(), b)
        r = scale_r[b][:, 0:1]
        a, up = act[b, :, :hid], act[b, :, hid:]
        sig = jax.nn.sigmoid(a)
        da = (r * (dh * up * sig * (1.0 + a * (1.0 - sig)))).astype(BF16)
        db = (r * (dh * a * sig)).astype(BF16)
        mixed = r * jnp.sum(da.astype(F32) * a + db.astype(F32) * up, axis=1, keepdims=True)
        d_all[b, d, :, 0:hid] = da
        d_all[b, d, :, hid:pair] = db
        d_all[b, d, :, pair:] = row_column(mixed, chunk).astype(BF16)
        ag_step(1, *ag_d(), b)

    def to_sibling(way, b):
        rest = core_src.at[way, b, 1 - c]
        copy = rcopy(rest, core_dst.at[way, b], core_s.at[2 + way, b], core_r.at[2 + way, b], sibling)
        copy.start()
        ends.append(copy.wait_send)

    def halves_out(way, value, b):
        for i in range(2):
            core_src[way, b, i] = value[:, i * half : (i + 1) * half].astype(BF16).reshape(chips, rows, half)

    def project_down(b):
        ag_finish(*ag_h(), b)
        h = h_all[b].reshape(batch, hid)
        p = jnp.dot(h, w_down[...], preferred_element_type=F32)
        halves_out(0, p, b)
        to_sibling(0, b)

    def project_dn(b):
        ag_finish(*ag_d(), b)
        flat = d_all[b].reshape(batch, pair + LANES)
        mixed = jnp.sum(flat[:, pair:].astype(F32), axis=1, keepdims=True)
        q = jnp.dot(flat[:, :pair], w_pair[...], preferred_element_type=F32)
        xf = whole(x_all, b).astype(F32)
        q = q - xf * (mixed * (1.0 / (width * dp)))
        halves_out(1, q, b)
        to_sibling(1, b)

    def scatter_slabs(way, b):
        rest = core_dst.at[way, b]
        rcopy(rest, rest, core_s.at[2 + way, b], core_r.at[2 + way, b], sibling).wait_recv()
        both = core_src[way, b, c].astype(F32) + core_dst[way, b].astype(F32)
        slab_src[way, b] = both.astype(BF16)
        for j in range(1, chips):
            to = turn(k, j, chips)
            rcopy(
                slab_src.at[way, b, to], slab_dst.at[way, b, k], slab_s.at[way, b], slab_r.at[way, b], chip_at(j)
            ).start()
        seven = slab_dst.at[way, b, pl.ds(0, chips - 1)]
        ends.append(lambda: rcopy(seven, seven, slab_s.at[way, b], slab_r.at[way, b], z_at(1)).wait_send())

    def slab_total(way, b):
        seven = slab_dst.at[way, b, pl.ds(0, chips - 1)]
        rcopy(seven, seven, slab_s.at[way, b], slab_r.at[way, b], z_at(1)).wait_recv()
        total = slab_src[way, b, k].astype(F32)
        for j in range(1, chips):
            total = total + slab_dst[way, b, turn(k, j, chips)].astype(F32)
        return total

    def finish_slab(way, value, into, b):
        row_src[way, b] = value.astype(BF16)
        if into is not None:
            for j in range(chips):
                rcopy(
                    row_src.at[way, b], into.at[b, c, k], row_s.at[way, b], bcast_r.at[way, b],
                    at(section=other, **chip_at(j)),
                ).start()
            eight = into.at[b, c]
            ends.append(lambda: rcopy(eight, eight, row_s.at[way, b], bcast_r.at[way, b], z_at(1)).wait_send())
        source = d * 2 + c
        crossed = rcopy(
            row_src.at[way, b], out_dst.at[way, source], out_s.at[way, b, 1], out_r.at[way], {"dp": b, **sibling}
        )
        crossed.start()
        ends.append(crossed.wait_send)
        copy = rcopy(row_src.at[way, b], out_dst.at[way, source], out_s.at[way, b, 0], out_r.at[way], at(dp=b))

        @pl.when(d == b)
        def _():
            out_dst[way, source] = row_src[way, b]

        @pl.when(d != b)
        def _():
            copy.start()

        def end():
            @pl.when(d != b)
            def _():
                copy.wait_send()

        ends.append(end)

    def finish_out(into, b):
        finish_slab(0, x_all[b, c, k].astype(F32) + slab_total(0, b), into, b)

    def finish_grad(into, b):
        finish_slab(1, g_all[b, c, k].astype(F32) + slab_total(1, b), into, b)

    def weight_grads(b):
        if b % 2 == 0:
            return
        x = whole(x_all, b - 1, 2)
        g = whole(g_all, b - 1, 2)
        pair_part = dot_tn(d_all[b - 1 : b + 1].reshape(2 * batch, pair + LANES)[:, :pair], x)
        down_part = dot_tn(h_all[b - 1 : b + 1].reshape(2 * batch, hid), g)
        if b == 1:
            acc_pair[...] = pair_part
            acc_down[...] = down_part
        else:
            acc_pair[...] += pair_part
            acc_down[...] += down_part

    def collect(way, ref):
        rest = out_dst.at[way, pl.ds(0, 2 * dp - 1)]
        rcopy(rest, rest, out_s.at[way, 0, 0], out_r.at[way], z_at(1)).wait_recv()
        for source in range(2 * dp):
            block = out_dst[way, source].astype(F32)
            ref[:, source * half : (source + 1) * half] = jnp.where(c == 0, block[: rows // 2], block[rows // 2 :])

    def part(function, *args):
        return functools.partial(function, *args)

    def wait_weights():
        for load in loads:
            load.wait()

    def close():
        scale = 1.0 / math.sqrt(tokens)
        gg_ref[...] = (acc_pair[0:hid] * scale).astype(BF16)
        gu_ref[...] = (acc_pair[hid:pair] * scale).astype(BF16)
        gd_ref[...] = (acc_down[...] * scale).astype(BF16)
        collect(0, out_ref)
        collect(1, grad_ref)
        for end in ends:
            end()
        ends.clear()

    def run(order, kinds, x_slabs, g_slabs, feed_op, hidden_op, out_op, grad_op):
        routes.update(kinds)
        ops = [
            feed_op,
            part(slabs_to_core, 0, x_all, x_slabs),
            project_up,
            *[part(rs_step, step, *rs_u()) for step in (2, 3, 4)],
            hidden_op,
            *[part(ag_step, step, *ag_h()) for step in (1, 2, 3, 4)],
            project_down,
            part(scatter_slabs, 0),
            out_op,
            part(slabs_to_core, 1, g_all, g_slabs),
            project_dh,
            *[part(rs_step, step, *rs_v()) for step in (2, 3, 4)],
            hidden_grad,
            *[part(ag_step, step, *ag_d()) for step in (2, 3, 4)],
            project_dn,
            part(scatter_slabs, 1),
            grad_op,
            weight_grads,
        ]
        for op, b in order:
            ops[op](b)

    @pl.when(sec == 0)
    def _():
        feed_all(x_all)
        wait_weights()
        run(
            ORDER_FIRST, ROUTES_FIRST, chips - 1, chips, part(feed_slab, 0, x_all), part(hidden, True),
            part(finish_out, x_all), part(finish_grad, None),
        )
        close()

    @pl.when(sec == 1)
    def _():
        feed_all(g_all)
        wait_weights()
        run(
            ORDER_SECOND, ROUTES_SECOND, chips, chips - 1, part(feed_slab, 1, g_all), part(hidden, False),
            part(finish_out, None), part(finish_grad, g_all),
        )
        close()


def finish_kernel(out_in, grad_in, gg_in, gu_in, gd_in, out_ref, grad_ref, gg_ref, gu_ref, gd_ref):
    share = out_ref.shape[2]
    for src, dst in ((out_in, out_ref), (grad_in, grad_ref)):
        for m in range(out_ref.shape[1]):
            dst[0, m] = src[m * share : (m + 1) * share].astype(BF16)
    for src, dst in ((gg_in, gg_ref), (gu_in, gu_ref), (gd_in, gd_ref)):
        dst[0] = src[...]


def shards(inputs, cotangent, gate_weight, up_weight, down_weight):
    first = lax.axis_index("section") == 0
    dp, tensors = lax.axis_size("dp"), lax.axis_size("tensor")
    micro, tok_dev, model = inputs.shape
    _, hid, width = gate_weight.shape
    chips = tensors // 2
    share = tok_dev // tensors
    held = micro * share
    nb, rows, half = dp, 2 * held, width // 2
    chunk = chips * rows // dp
    pair = 2 * hid
    tensor = lax.axis_index("tensor")
    start = tensor // 2 * (2 * share)
    pick = jnp.where(
        first,
        lax.dynamic_slice_in_dim(inputs, start, 2 * share, 1),
        lax.dynamic_slice_in_dim(cotangent, start, 2 * share, 1),
    )
    pick = pick.reshape(micro, 2, share, dp, 2, half)
    pick = jnp.where(tensor % 2 == 0, pick[:, :, :, :, 0], pick[:, :, :, :, 1])
    feed = pick.transpose(3, 1, 0, 2, 4).reshape(dp, rows, half)

    def sems(*shape):
        return pltpu.SemaphoreType.DMA(shape)

    def bf16(*shape):
        return pltpu.VMEM(shape, BF16)

    def f32(*shape):
        return pltpu.VMEM(shape, F32)

    sizes = (nb, dp, chips, rows, width, hid, micro * tok_dev * dp)
    vmem = pl.BlockSpec(memory_space=pltpu.VMEM)
    anywhere = pl.BlockSpec(memory_space=pl.ANY)
    out, grad, grad_gate, grad_up, grad_down = pl.pallas_call(
        functools.partial(kernel, sizes),
        out_shape=[
            jax.ShapeDtypeStruct((held, model), F32),
            jax.ShapeDtypeStruct((held, model), F32),
            jax.ShapeDtypeStruct((hid, width), BF16),
            jax.ShapeDtypeStruct((hid, width), BF16),
            jax.ShapeDtypeStruct((hid, width), BF16),
        ],
        in_specs=[vmem, anywhere, anywhere, anywhere],
        out_specs=[vmem] * 5,
        scratch_shapes=[
            bf16(pair, width),
            bf16(hid, width),
            bf16(nb, 2, chips, rows, half),
            bf16(nb, 2, chips, rows, half),
            f32(nb, dp, chunk, pair + LANES),
            bf16(nb, 2, 4, chunk, pair + LANES),
            bf16(nb, 2, 4, chunk, pair + LANES),
            f32(nb, dp, chunk, hid),
            bf16(nb, 2, 4, chunk, hid),
            bf16(nb, 2, 4, chunk, hid),
            f32(nb, chunk, pair),
            f32(nb, chunk, LANES),
            bf16(nb, dp, chunk, hid),
            bf16(nb, dp, chunk, pair + LANES),
            bf16(2, nb, 2, chips, rows, half),
            bf16(2, nb, chips, rows, half),
            bf16(2, nb, chips, rows, half),
            bf16(2, nb, chips, rows, half),
            bf16(2, nb, rows, half),
            bf16(2, 2 * dp, rows, half),
            f32(pair, width),
            f32(hid, width),
            sems(3),
            sems(1),
            sems(dp),
            sems(2, nb),
            sems(2, nb),
            sems(4, nb),
            sems(4, nb),
            *[sems(nb, 2, 4) for _ in range(8)],
            sems(2, nb),
            sems(2, nb),
            sems(2, nb),
            sems(2, nb, 2),
            sems(2),
        ],
        compiler_params=pltpu.CompilerParams(
            collective_id=0, has_side_effects=True, vmem_limit_bytes=56 * 1024 * 1024
        ),
    )(feed, gate_weight[0], up_weight[0], down_weight[0])
    return pl.pallas_call(
        finish_kernel,
        out_shape=[
            jax.ShapeDtypeStruct((1, micro, share, model), BF16),
            jax.ShapeDtypeStruct((1, micro, share, model), BF16),
            jax.ShapeDtypeStruct((1, hid, width), BF16),
            jax.ShapeDtypeStruct((1, hid, width), BF16),
            jax.ShapeDtypeStruct((1, hid, width), BF16),
        ],
        in_specs=[vmem] * 5,
        out_specs=[vmem] * 5,
    )(out, grad, grad_gate, grad_up, grad_down)


def solution(mesh):
    in_specs = (
        P(None, "dp", None),
        P(None, "dp", None),
        P("section", "tensor", "dp"),
        P("section", "tensor", "dp"),
        P("section", "tensor", "dp"),
    )
    out_specs = (
        P("section", None, ("dp", "tensor"), None),
        P("section", None, ("dp", "tensor"), None),
        P("section", "tensor", "dp"),
        P("section", "tensor", "dp"),
        P("section", "tensor", "dp"),
    )
    return jax.shard_map(shards, mesh=mesh, in_specs=in_specs, out_specs=out_specs, check_vma=False)
```

time: 195 us -> 172 us (0.88)
  Pallas kernels: 185 us -> 168 us
  local copies, waits for them, and re-layouts: 5.65 us -> 1.08 us
    pallas_call x1, Pallas kernels: 185 us -> 165 us  [shards(): pl.pallas_call(functools.partial(kernel, sizes), out_shape=[jax.ShapeDtyp...]
    unnamed x7 -> x0, local copies, waits for them, and re-layouts: 3.55 us -> none
    pallas_call x0 -> x1, Pallas kernels: none -> 2.9 us  [shards(): pl.pallas_call(finish_kernel, out_shape=[jax.ShapeDtypeStruct((1, micro,...]
where the time goes in v2:
time: 172 us; the launch traced here: 171 us
  Pallas kernels  168 us (98%)
    pallas_call x1, Pallas kernels, shards(): pl.pallas_call(functools.partial(kernel, sizes), out_shape=[jax.ShapeDtyp...  165 us

profile of v2, /device:TPU:1, one launch (start us, length us, event | category | flops | bytes accessed | tf_op | source)
XLA Modules:
  0.0 171.0 jit_solution(17824789342923541823)
XLA Ops:
  0.7 1.1 dynamic-slice_select_fusion
  1.7 0.1 reshape.18
  1.9 0.3 fusion.1
  2.2 0.1 fusion
  2.2 0.7 reshape.19.feed
  2.9 165.2 %shard_map.92 = (f32[8,6144]{1,0:T(8,128)}, f32[8,6144]{1,0:T(8,128)}, bf16[384,768]{1,0:T(8,128)(2,1)}, bf16[384,768]{1,0:T(8,128)(2,1)}, bf16[384,768]{1,0:T(8,128)(2,1)}) custom-call(bf16[8,16,384]{2,1,0:T(8,128)(2,1)} %reshape.19.feed, bf16[384,768]{1,0:T(8,128)(2,1)} %bitcast.7, bf16[384,768]{1,0:T(8,128)(2,1)} %bitcast.8, bf16[384,768]{1,0:T(8,128)(2,1)} %bitcast.9), custom_call_target="tpu_custom_call" | custom-call | tf_op jit(solution)/shard_map/pallas_call | solution.py:533
  168.1 2.9 %shard_map.93 = (bf16[1,2,4,6144]{3,2,1,0:T(4,128)(2,1)}, bf16[1,2,4,6144]{3,2,1,0:T(4,128)(2,1)}, bf16[1,384,768]{2,1,0:T(8,128)(2,1)}, bf16[1,384,768]{2,1,0:T(8,128)(2,1)}, bf16[1,384,768]{2,1,0:T(8,128)(2,1)}) custom-call(f32[8,6144]{1,0:T(8,128)} %get-tuple-element.10.out_in, f32[8,6144]{1,0:T(8,128)} %get-tuple-element.11.grad_in, ...), custom_call_target="tpu_custom_call" | custom-call | tf_op jit(solution)/shard_map/pallas_call | solution.py:585

commit v3 on v2

--- a/solution.py
+++ b/solution.py
@@ -55,8 +55,8 @@
     return lax.dot_general(a, b, (((0,), (0,)), ((), ())), preferred_element_type=F32)
 
 
-RING, PAIRS, DIRECT = 0, 1, 2
-PARENT = ((0, 1, 2, 3), (0, 0, 2, 2), (0, 0, 0, 0))
+RING, PAIRS, DIRECT, SHORT = 0, 1, 2, 3
+PARENT = ((0, 1, 2, 3), (0, 0, 2, 2), (0, 0, 0, 0), (0, 1, 2, 2))
 ROUTES_FIRST = {
     "u": (RING,) * 8,
     "h": (DIRECT,) * 8,
@@ -82,6 +82,8 @@
             some = [count + 1 - stage]
         elif kind == PAIRS:
             some = [(3, 4, 1), (2,)][stage - 1]
+        elif kind == SHORT:
+            some = [(4, 3), (2,), (1,)][stage - 1]
         else:
             some = (3, 4, 2, 1)
         pairs += [(way, s) for s in some if 1 <= s <= count]
@@ -93,7 +95,7 @@
 
 
 def waited(kind, s):
-    return (kind == RING and s <= 3) or (kind == PAIRS and s == 2)
+    return (kind == RING and s <= 3) or (kind == PAIRS and s == 2) or (kind == SHORT and s <= 2)
 
 
 def row_column(value, rows):
@@ -110,7 +112,7 @@
     part_u, send_u, recv_u, part_v, send_v, recv_v,
     act, scale_r, h_all, d_all,
     core_src, core_dst, slab_src, slab_dst, row_src, out_dst,
-    acc_pair, acc_down,
+    acc_pair, acc_down, stage_pair, stage_down,
     w_sem, feed_s, feed_r, bcast_s, bcast_r, core_s, core_r,
     rsu_s, rsu_r, rsv_s, rsv_r, agh_s, agh_r, agd_s, agd_r,
     slab_s, slab_r, row_s, out_s, out_r,
@@ -153,6 +155,11 @@
     ]
     for load in loads:
         load.start()
+    stores = [
+        pltpu.make_async_copy(stage_pair.at[pl.ds(0, hid)], gg_ref, w_sem.at[3]),
+        pltpu.make_async_copy(stage_pair.at[pl.ds(hid, hid)], gu_ref, w_sem.at[4]),
+        pltpu.make_async_copy(stage_down, gd_ref, w_sem.at[5]),
+    ]
 
     barrier = pltpu.get_barrier_semaphore()
     for j in range(1, dp):
@@ -412,9 +419,15 @@
         if b == 1:
             acc_pair[...] = pair_part
             acc_down[...] = down_part
-        else:
+        elif b < nb - 1:
             acc_pair[...] += pair_part
             acc_down[...] += down_part
+        else:
+            scale = 1.0 / math.sqrt(tokens)
+            stage_pair[...] = ((acc_pair[...] + pair_part) * scale).astype(BF16)
+            stage_down[...] = ((acc_down[...] + down_part) * scale).astype(BF16)
+            for store in stores:
+                store.start()
 
     def collect(way, ref):
         rest = out_dst.at[way, pl.ds(0, 2 * dp - 1)]
@@ -431,14 +444,12 @@
             load.wait()
 
     def close():
-        scale = 1.0 / math.sqrt(tokens)
-        gg_ref[...] = (acc_pair[0:hid] * scale).astype(BF16)
-        gu_ref[...] = (acc_pair[hid:pair] * scale).astype(BF16)
-        gd_ref[...] = (acc_down[...] * scale).astype(BF16)
         collect(0, out_ref)
         collect(1, grad_ref)
         for end in ends:
             end()
+        for store in stores:
+            store.wait()
         ends.clear()
 
     def run(order, kinds, x_slabs, g_slabs, feed_op, hidden_op, out_op, grad_op):
@@ -540,7 +551,7 @@
             jax.ShapeDtypeStruct((hid, width), BF16),
         ],
         in_specs=[vmem, anywhere, anywhere, anywhere],
-        out_specs=[vmem] * 5,
+        out_specs=[vmem, vmem, anywhere, anywhere, anywhere],
         scratch_shapes=[
             bf16(pair, width),
             bf16(hid, width),
@@ -564,7 +575,9 @@
             bf16(2, 2 * dp, rows, half),
             f32(pair, width),
             f32(hid, width),
-            sems(3),
+            bf16(pair, width),
+            bf16(hid, width),
+            sems(6),
             sems(1),
             sems(dp),
             sems(2, nb),

time: 172 us -> 171 us (level)
  no operation moved by 1% of the time
where the time goes in v3:
time: 171 us; the launch traced here: 170 us
  Pallas kernels  167 us (98%)
    pallas_call x1, Pallas kernels, shards(): pl.pallas_call(functools.partial(kernel, sizes), out_shape=[jax.ShapeDtyp...  164 us

profile of v3, /device:TPU:1, one launch (start us, length us, event | category | flops | bytes accessed | tf_op | source)
XLA Modules:
  0.0 170.0 jit_solution(13260864222043592285)
XLA Ops:
  0.7 1.1 dynamic-slice_select_fusion
  1.7 0.1 reshape.18
  1.9 0.3 fusion.1
  2.2 0.1 fusion
  2.2 0.7 reshape.19.feed
  2.9 164.2 %shard_map.92 = (f32[8,6144]{1,0:T(8,128)}, f32[8,6144]{1,0:T(8,128)}, bf16[384,768]{1,0:T(8,128)(2,1)}, bf16[384,768]{1,0:T(8,128)(2,1)}, bf16[384,768]{1,0:T(8,128)(2,1)}) custom-call(bf16[8,16,384]{2,1,0:T(8,128)(2,1)} %reshape.19.feed, bf16[384,768]{1,0:T(8,128)(2,1)} %bitcast.7, bf16[384,768]{1,0:T(8,128)(2,1)} %bitcast.8, bf16[384,768]{1,0:T(8,128)(2,1)} %bitcast.9), custom_call_target="tpu_custom_call" | custom-call | tf_op jit(solution)/shard_map/pallas_call | solution.py:544
  167.1 2.9 %shard_map.93 = (bf16[1,2,4,6144]{3,2,1,0:T(4,128)(2,1)}, bf16[1,2,4,6144]{3,2,1,0:T(4,128)(2,1)}, bf16[1,384,768]{2,1,0:T(8,128)(2,1)}, bf16[1,384,768]{2,1,0:T(8,128)(2,1)}, bf16[1,384,768]{2,1,0:T(8,128)(2,1)}) custom-call(f32[8,6144]{1,0:T(8,128)} %get-tuple-element.10.out_in, f32[8,6144]{1,0:T(8,128)} %get-tuple-element.11.grad_in, ...), custom_call_target="tpu_custom_call" | custom-call | tf_op jit(solution)/shard_map/pallas_call | solution.py:598
